TPU v7x, 512 devices: a whole 4x8x8 slice. The times are simulated.
512 devices in a mesh: space: 16 (over z, core), member: 8 (over y), tm: 4 (over x).
Axes of the slice: x: 4, y: 8, z: 8, core: 2. Of those that a mesh axis runs over, the one named last changes fastest.
Arguments:
- ens_pert: bfloat16 [8, 128, 131072], P('tm', 'member', 'space'), may hold values from -6 to 6
- weights: float32 [128, 512], P('member', 'space'), may hold values from -6 to 6
- foot_block: int32 [8, 16, 16, 8, 32], P('tm', 'space'), may hold values from 0 to 31
- foot_offset: int32 [8, 16, 16, 8, 32], P('tm', 'space'), may hold values from 0 to 255
- innovation: float32 [8, 16, 8, 16, 32], P('tm', 'space', 'member'), may hold values from -6 to 6
- inv_var: float32 [8, 16, 8, 16, 32], P('tm', 'space', 'member'), may hold values from 0.25 to 2.5
- obs_count: int32 [8, 16, 8, 16], P('tm', 'space', 'member'), may hold values from 1 to 32, as said below
Outputs:
- gradient: float32 [128, 512], P('member', 'space')
Inputs may be any that keep to these rules, and one draw needn't show every extreme that they name: `obs_count`: live slots come first among the 32 slots; in every time slot one destination tile has all 32 slots live from every owner.
All inputs are finite; a program needn't handle non-finite values.
Results may differ from a plain program's by a relative error of at most 0.0029.
Values sent between devices are 32-bit elements; how exact they have to be, the bound alone decides.
No kernel may reach another device: no remote copies, remote signals or barrier semaphores. Data moves between devices by JAX's collectives and lax.ppermute only.
A program may use at most 64 MiB of HBM per device.

v0:
```python
import math
import jax
import jax.numpy as jnp
from jax import lax
from jax.sharding import PartitionSpec as P

BLOCK = 256


def split_pair(values, axis_at):
    upper = lax.optimization_barrier(values.astype(jnp.bfloat16))
    lower = (values - upper.astype(jnp.float32)).astype(jnp.bfloat16)
    return jnp.concatenate([upper, lower], axis=axis_at)


def shards(ens_pert, weights, foot_block, foot_offset, innovation, inv_var, obs_count):
    tile_count = lax.axis_size("space")
    group_count = lax.axis_size("member")
    slot_count, members, cell_dev = ens_pert.shape
    capacity = foot_block.shape[-1]
    blk_dev = cell_dev // BLOCK
    norm_scale = 1.0 / math.sqrt(members * group_count - 1)
    pert_blocks = ens_pert.reshape(slot_count, members, blk_dev, BLOCK)
    weights_rounded = weights.astype(jnp.bfloat16)
    partial_field = norm_scale * jnp.einsum(
        "tmbc,mb->tbc", pert_blocks, weights_rounded, preferred_element_type=jnp.float32
    )
    split_field = split_pair(partial_field, 1)
    block_rows = jnp.transpose(foot_block.reshape(slot_count, tile_count, -1), (1, 0, 2))
    offset_rows = jnp.transpose(foot_offset.reshape(slot_count, tile_count, -1), (1, 0, 2))
    block_iota = lax.broadcasted_iota(jnp.int32, (1, blk_dev, 1), 1)
    offset_iota = lax.broadcasted_iota(jnp.int32, (1, 1, BLOCK), 2)

    def pick_tile(pair):
        blk_ids, off_ids = pair
        off_hot = (off_ids[:, :, None] == offset_iota).astype(jnp.bfloat16)
        proj = jnp.einsum("tjc,tkc->tjk", split_field, off_hot, preferred_element_type=jnp.float32)
        value = proj[:, :blk_dev] + proj[:, blk_dev:]
        chosen = jnp.where(blk_ids[:, None, :] == block_iota, value, jnp.zeros_like(value))
        return jnp.sum(chosen, axis=1)

    picked = jnp.transpose(lax.map(pick_tile, (block_rows, offset_rows)), (1, 0, 2))
    arrived_vals = lax.all_to_all(
        picked.reshape(slot_count, tile_count * group_count, capacity),
        ("space", "member"),
        split_axis=1,
        concat_axis=1,
        tiled=True,
    )
    model_obs = jnp.sum(arrived_vals.reshape(slot_count, tile_count, group_count, capacity), axis=2)
    innov_local = innovation.reshape(slot_count, tile_count, capacity)
    obs_weight = inv_var.reshape(slot_count, tile_count, capacity)
    counts = obs_count.reshape(slot_count, tile_count, 1)
    is_live = lax.broadcasted_iota(jnp.int32, (slot_count, tile_count, capacity), 2) < counts
    residual = jnp.where(
        is_live, obs_weight * (model_obs - innov_local), jnp.zeros_like(innov_local)
    )
    residual = residual.reshape(slot_count, 1, 1, tile_count, capacity)
    spread = lax.all_gather(residual, "member", axis=2, tiled=True)
    arrived = lax.all_to_all(spread, "space", split_axis=3, concat_axis=1, tiled=True)
    arrived_rows = jnp.transpose(arrived.reshape(slot_count, tile_count, -1), (1, 0, 2))

    def add_tile(total, triple):
        blk_ids, off_ids, values = triple
        off_hot = (off_ids[:, :, None] == offset_iota).astype(jnp.bfloat16)
        placed = jnp.where(
            blk_ids[:, None, :] == block_iota, values[:, None, :], jnp.zeros((), jnp.float32)
        )
        both = split_pair(placed, 1)
        part_sum = jnp.einsum("tjk,tkc->tjc", both, off_hot, preferred_element_type=jnp.float32)
        return (total + (part_sum[:, :blk_dev] + part_sum[:, blk_dev:]), None)

    start_total = jnp.zeros((slot_count, blk_dev, BLOCK), jnp.float32)
    adjoint, _ = lax.scan(add_tile, start_total, (block_rows, offset_rows, arrived_rows))
    adjoint_rounded = adjoint.astype(jnp.bfloat16)
    local_grad = jnp.einsum(
        "tmbc,tbc->mb", pert_blocks, adjoint_rounded, preferred_element_type=jnp.float32
    )
    summed = lax.psum(local_grad, "tm")
    return weights + norm_scale * summed


def solution(mesh):
    in_specs = (
        P("tm", "member", "space"),
        P("member", "space"),
        P("tm", "space", None, None, None),
        P("tm", "space", None, None, None),
        P("tm", "space", "member", None, None),
        P("tm", "space", "member", None, None),
        P("tm", "space", "member", None),
    )
    out_specs = P("member", "space")
    return jax.shard_map(shards, mesh=mesh, in_specs=in_specs, out_specs=out_specs, check_vma=False)
```

profile of v0, /device:TPU:1, one launch (start us, length us, event | category | flops | bytes accessed | tf_op | source)
XLA Modules:
  0.0 95.3 jit_solution(16273810836954491873)
XLA Ops:
  0.0 0.7 convert_bitcast_fusion.1
  0.8 1.2 %fusion.21 = f32[32,1,2,256]{3,1,2,0:T(1,128)S(1)} fusion(bf16[16,32,1,1]{0,2,3,1:T(2,128)(2,1)S(1)} %copy.38, bf16[2,2,32,8,256]{4,3,2,1,0:T(8,128)(2,1)} %bitcast.84), kind=kOutput, calls=%fused_computation.32 | convolution fusion | flops 524288 | bytes 590848 | tf_op jit(solution)/shard_map/tmbc,mb->tbc/dot_general | solution.py:25
  2.1 0.8 copy-done.1
  3.2 5.8 %while.22 = (s32[]{:T(128)}, f32[16,2,256]{2,1,0:T(2,128)S(1)}, s32[16,2,256]{2,1,0:T(2,128)S(1)}, s32[16,2,256]{2,1,0:T(2,128)S(1)}, bf16[2,64,256]{2,1,0:T(8,128)(2,1)S(1)}, /*index=5*/s32[]{:T(128)}) while((s32[]{:T(128)}, f32[16,2,256]{2,1,0:T(2,128)S(1)}, s32[16,2,256]{2,1,0:T(2,128)S(1)}, s32[16,2,256]{2,1,0:T(2,128)S(1)}, ...), condition=%wide.region_2.3_spmd.clone, body=%wide.region_0.2_spmd.clone.sunk | while | flops 16973312 | bytes 346189 | solution.py:42
  9.1 0.8 copy.33
  9.9 18.4 %all-to-all-start = ((f32[2,128,32]{2,0,1:T(2,128)}), f32[2,128,32]{2,0,1:T(2,128)S(1)}, u32[]{:S(2)}, u32[]{:S(2)}) async-start(f32[2,128,32]{2,0,1:T(2,128)} %copy.33), calls=%async_computation | async-start | bytes 262144 | tf_op jit(solution)/shard_map/all_to_all | solution.py:43
  28.3 0.7 copy-done.6
  29.1 11.8 %all-to-all-done = f32[2,128,32]{2,0,1:T(2,128)S(1)} async-done(((f32[2,128,32]{2,0,1:T(2,128)}), f32[2,128,32]{2,0,1:T(2,128)S(1)}, u32[]{:S(2)}, u32[]{:S(2)}) %all-to-all-start) | async-done | bytes 32800 | tf_op jit(solution)/shard_map/all_to_all | solution.py:43
  41.0 18.2 %all_gather.3 = f32[2,1,8,16,32]{4,3,1,0,2:T(8,128)S(1)} all-gather(f32[2,1,1,16,32]{4,3,1,0,2:T(8,128)S(1)} %copy.36), channel_id=1, replica_groups=mesh['space'=16,'member'=8,'tm'=4] {'member'}, dimensions={2}, use_global_device_ids=true | all-gather | bytes 36864 | tf_op jit(solution)/shard_map/all_gather | solution.py:59
  59.4 0.7 reshape.54
  60.1 10.0 %all-to-all-start.1 = ((f32[16,1,512]{2,1,0:T(1,128)}), f32[16,1,512]{2,1,0:T(1,128)S(1)}, u32[]{:S(2)}, u32[]{:S(2)}) async-start(f32[16,1,512]{2,1,0:T(1,128)} %reshape.54), calls=%async_computation.1 | async-start | bytes 65536 | tf_op jit(solution)/shard_map/all_to_all | solution.py:60
  70.1 7.5 %all-to-all-done.1 = f32[16,1,512]{2,1,0:T(1,128)S(1)} async-done(((f32[16,1,512]{2,1,0:T(1,128)}), f32[16,1,512]{2,1,0:T(1,128)S(1)}, u32[]{:S(2)}, u32[]{:S(2)}) %all-to-all-start.1) | async-done | bytes 32800 | tf_op jit(solution)/shard_map/all_to_all | solution.py:60
  77.6 0.5 broadcast.27
  78.1 0.7 reduce
  79.0 6.6 %while.23 = (s32[]{:T(128)}, f32[2,32,256]{2,1,0:T(8,128)S(1)}, s32[16,2,256]{2,1,0:T(2,128)S(1)}, f32[16,2,256]{2,1,0:T(2,128)S(1)}, s32[16,2,256]{2,1,0:T(2,128)S(1)}, /*index=5*/s32[]{:T(128)}, s32[]{:T(128)}) while((s32[]{:T(128)}, f32[2,32,256]{2,1,0:T(8,128)S(1)}, s32[16,2,256]{2,1,0:T(2,128)S(1)}, ...), condition=%wide.region_5.6_spmd.clone, body=%wide.region_4.5_spmd.clone.sunk | while | flops 17203200 | bytes 579679 | solution.py:74
  79.1 0.3 fusion.40
  83.2 0.3 fusion.40
  83.7 0.3 fusion.40
  84.1 0.3 fusion.40
  84.5 0.3 fusion.40
  84.9 0.3 fusion.40
  85.3 0.3 fusion.40
  86.0 8.7 %psum.7 = f32[16,32]{1,0:T(8,128)S(1)} all-reduce(f32[16,32]{1,0:T(8,128)S(1)} %bitcast.88), channel_id=1, replica_groups=mesh['space'=16,'member'=8,'tm'=4] {'tm'}, use_global_device_ids=true, to_apply=%region_6.7 | all-reduce | flops 512 | bytes 4096 | tf_op jit(solution)/shard_map/psum | solution.py:79
  94.7 0.6 multiply_add_fusion
  (187 shorter events, 10.2 us)
Async XLA Ops:
  2.1 0.9 copy-start.1
  2.1 1.0 %copy-start.2 = (s32[2,1,16,8,32]{4,3,2,1,0:T(8,128)S(1)}, s32[2,1,16,8,32]{4,3,2,1,0:T(8,128)}, u32[]{:S(2)}) copy-start(s32[2,1,16,8,32]{4,3,2,1,0:T(8,128)} %param.14) | copy-start | bytes 98308
  9.9 31.0 %all-to-all-start = ((f32[2,128,32]{2,0,1:T(2,128)}), f32[2,128,32]{2,0,1:T(2,128)S(1)}, u32[]{:S(2)}, u32[]{:S(2)}) async-start(f32[2,128,32]{2,0,1:T(2,128)} %copy.33), calls=%async_computation | async-start | bytes 262144 | tf_op jit(solution)/shard_map/all_to_all | solution.py:43
  28.3 0.7 copy-start.6
  29.1 11.8 %copy-start.4 = (f32[2,1,1,16,32]{4,3,2,1,0:T(8,128)S(1)}, f32[2,1,1,16,32]{4,3,2,1,0:T(8,128)}, u32[]{:S(2)}) copy-start(f32[2,1,1,16,32]{4,3,2,1,0:T(8,128)} %param.16) | copy-start | bytes 12292
  29.1 11.8 %copy-start.5 = (f32[2,1,1,16,32]{4,3,2,1,0:T(8,128)S(1)}, f32[2,1,1,16,32]{4,3,2,1,0:T(8,128)}, u32[]{:S(2)}) copy-start(f32[2,1,1,16,32]{4,3,2,1,0:T(8,128)} %param.15) | copy-start | bytes 12292
  60.1 17.5 %all-to-all-start.1 = ((f32[16,1,512]{2,1,0:T(1,128)}), f32[16,1,512]{2,1,0:T(1,128)S(1)}, u32[]{:S(2)}, u32[]{:S(2)}) async-start(f32[16,1,512]{2,1,0:T(1,128)} %reshape.54), calls=%async_computation.1 | async-start | bytes 65536 | tf_op jit(solution)/shard_map/all_to_all | solution.py:60
  79.0 6.6 %copy-start = (bf16[2,16,8192]{2,1,0:T(8,128)(2,1)S(1)}, bf16[2,16,8192]{2,1,0:T(8,128)(2,1)}, u32[]{:S(2)}) copy-start(bf16[2,16,8192]{2,1,0:T(8,128)(2,1)} %param.11) | copy-start | bytes 1572868
  86.0 8.7 %copy-start.3 = (f32[16,32]{1,0:T(8,128)S(1)}, f32[16,32]{1,0:T(8,128)}, u32[]{:S(2)}) copy-start(f32[16,32]{1,0:T(8,128)} %param.12) | copy-start | bytes 6148
where the time goes:
time: 95.7 us; the launch traced here: 95.3 us
  starting transfers between devices  28.4 us (30%)
  blocking collectives  26.9 us (28%)
  waiting for transfers between devices  19.2 us (20%)
  matrix products  10.3 us (11%)
  local copies, waits for them, and re-layouts  5.06 us (5%)
  other arithmetic  3.52 us (4%)
  loops' own time  1.59 us (2%)
    all_to_all x1, starting transfers between devices, shards(): lax.all_to_all(picked.reshape(slot_count, tile_count * group_count, capac...  18.4 us
    all_gather x1, blocking collectives, shards(): spread = lax.all_gather(residual, 'member', axis=2, tiled=True)  18.2 us
    all_to_all x1, waiting for transfers between devices, shards(): lax.all_to_all(picked.reshape(slot_count, tile_count * group_count, capac...  11.8 us
    all_to_all x1, starting transfers between devices, shards(): lax.all_to_all(spread, 'space', split_axis=3, concat_axis=1, tiled=True)  10 us
    psum x1, blocking collectives, shards(): summed = lax.psum(local_grad, 'tm')  8.7 us
    all_to_all x1, waiting for transfers between devices, shards(): lax.all_to_all(spread, 'space', split_axis=3, concat_axis=1, tiled=True)  7.48 us
    dot_general x16, matrix products, add_tile(): jnp.einsum('tjk,tkc->tjc', both, off_hot, preferred_element_type=jnp.floa...  4.45 us
    dot_general x16, matrix products, pick_tile(): jnp.einsum('tjc,tkc->tjk', split_field, off_hot, preferred_element_type=j...  4.35 us
  transfers between devices with their start and end apart: 2, of which 2 were waited for; matrix products, arithmetic and copies ran while one was open for 0% of the time, Pallas kernels for 0%

commit v1 on v0

--- a/solution.py
+++ b/solution.py
@@ -56,7 +56,9 @@
         is_live, obs_weight * (model_obs - innov_local), jnp.zeros_like(innov_local)
     )
     residual = residual.reshape(slot_count, 1, 1, tile_count, capacity)
-    spread = lax.all_gather(residual, "member", axis=2, tiled=True)
+    spread = jnp.concatenate(
+        lax.all_to_all(jnp.stack([residual] * lax.axis_size("member")), "member", 0, 0), axis=2
+    )
     arrived = lax.all_to_all(spread, "space", split_axis=3, concat_axis=1, tiled=True)
     arrived_rows = jnp.transpose(arrived.reshape(slot_count, tile_count, -1), (1, 0, 2))
 

time: 95.7 us -> 83.1 us (0.87)
  blocking collectives: 26.9 us -> 17.9 us
  starting transfers between devices: 28.4 us -> 23.8 us
    all_gather x1 -> x0, blocking collectives: 18.2 us -> none  [shards(): spread = lax.all_gather(residual, 'member', axis=2, tiled=True)]
    all_to_all x0 -> x1, blocking collectives: none -> 9.25 us  [shards(): lax.all_to_all(jnp.stack([residual] * lax.axis_size('member')), 'member',...]
    all_to_all x1, starting transfers between devices: 10 us -> 5.34 us  [shards(): lax.all_to_all(spread, 'space', split_axis=3, concat_axis=1, tiled=True)]
    unnamed x16 -> x19, local copies, waits for them, and re-layouts: 2.36 us -> 2.71 us
where the time goes in v1:
time: 83.1 us; the launch traced here: 82.7 us
  starting transfers between devices  23.8 us (29%)
  waiting for transfers between devices  19.2 us (23%)
  blocking collectives  17.9 us (22%)
  matrix products  10.3 us (12%)
  local copies, waits for them, and re-layouts  5.42 us (7%)
  other arithmetic  4.19 us (5%)
  loops' own time  1.59 us (2%)
    all_to_all x1, starting transfers between devices, shards(): lax.all_to_all(picked.reshape(slot_count, tile_count * group_count, capac...  18.4 us
    all_to_all x1, waiting for transfers between devices, shards(): lax.all_to_all(picked.reshape(slot_count, tile_count * group_count, capac...  11.8 us
    all_to_all x1, blocking collectives, shards(): lax.all_to_all(jnp.stack([residual] * lax.axis_size('member')), 'member',...  9.25 us
    psum x1, blocking collectives, shards(): summed = lax.psum(local_grad, 'tm')  8.7 us
    all_to_all x1, waiting for transfers between devices, shards(): lax.all_to_all(spread, 'space', split_axis=3, concat_axis=1, tiled=True)  7.48 us
    all_to_all x1, starting transfers between devices, shards(): lax.all_to_all(spread, 'space', split_axis=3, concat_axis=1, tiled=True)  5.34 us
    dot_general x16, matrix products, add_tile(): jnp.einsum('tjk,tkc->tjc', both, off_hot, preferred_element_type=jnp.floa...  4.45 us
    dot_general x16, matrix products, pick_tile(): jnp.einsum('tjc,tkc->tjk', split_field, off_hot, preferred_element_type=j...  4.35 us
  transfers between devices with their start and end apart: 2, of which 2 were waited for; matrix products, arithmetic and copies ran while one was open for 0% of the time, Pallas kernels for 0%

profile of v1, /device:TPU:1, one launch (start us, length us, event | category | flops | bytes accessed | tf_op | source)
XLA Modules:
  0.0 82.7 jit_solution(11294219909348803974)
XLA Ops:
  0.0 0.7 convert_bitcast_fusion.1
  0.8 1.2 %fusion.21 = f32[32,1,2,256]{3,1,2,0:T(1,128)S(1)} fusion(bf16[16,32,1,1]{0,2,3,1:T(2,128)(2,1)S(1)} %copy.29, bf16[2,2,32,8,256]{4,3,2,1,0:T(8,128)(2,1)} %bitcast.94), kind=kOutput, calls=%fused_computation.32 | convolution fusion | flops 524288 | bytes 590848 | tf_op jit(solution)/shard_map/tmbc,mb->tbc/dot_general | solution.py:25
  2.1 0.8 %copy-done.1 = s32[2,1,16,8,32]{4,3,2,1,0:T(8,128)S(1)} copy-done((s32[2,1,16,8,32]{4,3,2,1,0:T(8,128)S(1)}, s32[2,1,16,8,32]{4,3,2,1,0:T(8,128)}, u32[]{:S(2)}) %copy-start.1) | copy-done | bytes 32792
  3.2 5.8 %while.22 = (s32[]{:T(128)}, f32[16,2,256]{2,1,0:T(2,128)S(1)}, s32[16,2,256]{2,1,0:T(2,128)S(1)}, s32[16,2,256]{2,1,0:T(2,128)S(1)}, bf16[2,64,256]{2,1,0:T(8,128)(2,1)S(1)}, /*index=5*/s32[]{:T(128)}) while((s32[]{:T(128)}, f32[16,2,256]{2,1,0:T(2,128)S(1)}, s32[16,2,256]{2,1,0:T(2,128)S(1)}, s32[16,2,256]{2,1,0:T(2,128)S(1)}, ...), condition=%wide.region_2.3_spmd.clone, body=%wide.region_0.2_spmd.clone.sunk | while | flops 16973312 | bytes 346189 | solution.py:42
  9.1 0.7 copy.25
  9.9 18.4 %all-to-all-start = ((f32[2,128,32]{2,0,1:T(2,128)}), f32[2,128,32]{2,0,1:T(2,128)S(1)}, u32[]{:S(2)}, u32[]{:S(2)}) async-start(f32[2,128,32]{2,0,1:T(2,128)} %copy.25), calls=%async_computation | async-start | bytes 262144 | tf_op jit(solution)/shard_map/all_to_all | solution.py:43
  28.3 0.7 copy-done.6
  29.1 11.8 %all-to-all-done = f32[2,128,32]{2,0,1:T(2,128)S(1)} async-done(((f32[2,128,32]{2,0,1:T(2,128)}), f32[2,128,32]{2,0,1:T(2,128)S(1)}, u32[]{:S(2)}, u32[]{:S(2)}) %all-to-all-start) | async-done | bytes 32800 | tf_op jit(solution)/shard_map/all_to_all | solution.py:43
  41.2 9.2 %all_to_all.25 = f32[8,1,1024]{2,1,0:T(1,128)S(1)} all-to-all(f32[8,1,1024]{2,1,0:T(1,128)S(1)} %reshape.67), channel_id=1, replica_groups=mesh['space'=16,'member'=8,'tm'=4] {'member'}, dimensions={0} | all-to-all | bytes 65536 | tf_op jit(solution)/shard_map/all_to_all | solution.py:60
  50.5 0.5 broadcast.31
  51.0 0.7 reduce
  52.0 0.7 reshape.69
  52.7 5.3 %all-to-all-start.2 = ((f32[16,1,512]{2,1,0:T(1,128)}), f32[16,1,512]{2,1,0:T(1,128)S(1)}, u32[]{:S(2)}, u32[]{:S(2)}) async-start(f32[16,1,512]{2,1,0:T(1,128)} %reshape.69), calls=%async_computation.2 | async-start | bytes 65536 | tf_op jit(solution)/shard_map/all_to_all | solution.py:62
  58.0 7.5 %all-to-all-done.2 = f32[16,1,512]{2,1,0:T(1,128)S(1)} async-done(((f32[16,1,512]{2,1,0:T(1,128)}), f32[16,1,512]{2,1,0:T(1,128)S(1)}, u32[]{:S(2)}, u32[]{:S(2)}) %all-to-all-start.2) | async-done | bytes 32800 | tf_op jit(solution)/shard_map/all_to_all | solution.py:62
  65.5 0.7 reduce.1
  66.4 6.6 %while.23 = (s32[]{:T(128)}, f32[2,32,256]{2,1,0:T(8,128)S(1)}, s32[16,2,256]{2,1,0:T(2,128)S(1)}, f32[16,2,256]{2,1,0:T(2,128)S(1)}, s32[16,2,256]{2,1,0:T(2,128)S(1)}, /*index=5*/s32[]{:T(128)}, s32[]{:T(128)}) while((s32[]{:T(128)}, f32[2,32,256]{2,1,0:T(8,128)S(1)}, s32[16,2,256]{2,1,0:T(2,128)S(1)}, ...), condition=%wide.region_5.6_spmd.clone, body=%wide.region_4.5_spmd.clone.sunk | while | flops 17203200 | bytes 579679 | solution.py:76
  69.0 0.3 fusion.41
  69.4 0.3 fusion.41
  69.8 0.3 fusion.41
  70.2 0.3 fusion.41
  70.6 0.3 fusion.41
  71.1 0.3 fusion.41
  73.4 8.7 %psum.7 = f32[16,32]{1,0:T(8,128)S(1)} all-reduce(f32[16,32]{1,0:T(8,128)S(1)} %bitcast.98), channel_id=1, replica_groups=mesh['space'=16,'member'=8,'tm'=4] {'tm'}, use_global_device_ids=true, to_apply=%region_6.7 | all-reduce | flops 512 | bytes 4096 | tf_op jit(solution)/shard_map/psum | solution.py:81
  82.1 0.6 multiply_add_fusion
  (191 shorter events, 10.8 us)
Async XLA Ops:
  2.1 0.9 %copy-start.1 = (s32[2,1,16,8,32]{4,3,2,1,0:T(8,128)S(1)}, s32[2,1,16,8,32]{4,3,2,1,0:T(8,128)}, u32[]{:S(2)}) copy-start(s32[2,1,16,8,32]{4,3,2,1,0:T(8,128)} %param.13) | copy-start | bytes 98308
  2.1 1.0 %copy-start.2 = (s32[2,1,16,8,32]{4,3,2,1,0:T(8,128)S(1)}, s32[2,1,16,8,32]{4,3,2,1,0:T(8,128)}, u32[]{:S(2)}) copy-start(s32[2,1,16,8,32]{4,3,2,1,0:T(8,128)} %param.14) | copy-start | bytes 98308
  9.9 31.0 %all-to-all-start = ((f32[2,128,32]{2,0,1:T(2,128)}), f32[2,128,32]{2,0,1:T(2,128)S(1)}, u32[]{:S(2)}, u32[]{:S(2)}) async-start(f32[2,128,32]{2,0,1:T(2,128)} %copy.25), calls=%async_computation | async-start | bytes 262144 | tf_op jit(solution)/shard_map/all_to_all | solution.py:43
  28.3 0.7 copy-start.6
  29.1 11.8 %copy-start.4 = (f32[2,1,1,16,32]{4,3,2,1,0:T(8,128)S(1)}, f32[2,1,1,16,32]{4,3,2,1,0:T(8,128)}, u32[]{:S(2)}) copy-start(f32[2,1,1,16,32]{4,3,2,1,0:T(8,128)} %param.16) | copy-start | bytes 12292
  29.1 11.8 %copy-start.5 = (f32[2,1,1,16,32]{4,3,2,1,0:T(8,128)S(1)}, f32[2,1,1,16,32]{4,3,2,1,0:T(8,128)}, u32[]{:S(2)}) copy-start(f32[2,1,1,16,32]{4,3,2,1,0:T(8,128)} %param.15) | copy-start | bytes 12292
  52.7 12.8 %all-to-all-start.2 = ((f32[16,1,512]{2,1,0:T(1,128)}), f32[16,1,512]{2,1,0:T(1,128)S(1)}, u32[]{:S(2)}, u32[]{:S(2)}) async-start(f32[16,1,512]{2,1,0:T(1,128)} %reshape.69), calls=%async_computation.2 | async-start | bytes 65536 | tf_op jit(solution)/shard_map/all_to_all | solution.py:62
  66.4 6.6 %copy-start = (bf16[2,16,8192]{2,1,0:T(8,128)(2,1)S(1)}, bf16[2,16,8192]{2,1,0:T(8,128)(2,1)}, u32[]{:S(2)}) copy-start(bf16[2,16,8192]{2,1,0:T(8,128)(2,1)} %param.11) | copy-start | bytes 1572868
  73.4 8.7 %copy-start.3 = (f32[16,32]{1,0:T(8,128)S(1)}, f32[16,32]{1,0:T(8,128)}, u32[]{:S(2)}) copy-start(f32[16,32]{1,0:T(8,128)} %param.12) | copy-start | bytes 6148
